TPU v7x, 32 devices: a whole 2x2x4 slice. The times are simulated.
32 devices in a mesh: expert: 8 (over z, y), shard: 4 (over x, core).
Axes of the slice: x: 2, y: 2, z: 4, core: 2. Of those that a mesh axis runs over, the one named last changes fastest.
Arguments:
- tokens: bfloat16 [8, 1024, 768], P('expert', 'shard'), may hold values from -6 to 6
- gain_attn: bfloat16 [768], P('shard'), may hold values from 0.5 to 1.5
- pos_table: bfloat16 [32, 12], P('shard'), may hold values from -4 to 4
- buckets: int32 [2047], replicated, may hold values from 0 to 31
- w_query: bfloat16 [768, 768], P('shard'), may hold values from -0.21875 to 0.21875
- w_key: bfloat16 [768, 768], P('shard'), may hold values from -0.21875 to 0.21875
- w_value: bfloat16 [768, 768], P('shard'), may hold values from -0.21875 to 0.21875
- w_attn_out: bfloat16 [768, 768], P('shard'), may hold values from -0.875 to 0.875
- w_router: bfloat16 [768, 8], P('shard'), may hold values from -0.109375 to 0.109375
- gain_ffn: bfloat16 [768], P('shard'), may hold values from 0.5 to 1.5
- w_in: bfloat16 [8, 768, 3072], P('expert', None, 'shard'), may hold values from -0.21875 to 0.21875
- w_out: bfloat16 [8, 3072, 768], P('expert', 'shard'), may hold values from -10 to 10
- expert_ids: int32 [8, 1024], P('expert', 'shard'), may hold values from 0 to 7, as said below
- slots: int32 [8, 1024], P('expert', 'shard'), may hold values from 0 to 3, as said below
- keep: int32 [8, 1024], P('expert', 'shard'), may hold values from 0 to 1, as said below
- grad_out: bfloat16 [8, 1024, 768], P('expert', 'shard'), may hold values from -6 to 6
Outputs:
- output: bfloat16 [8, 1024, 768], P('expert', 'shard')
- grad_tokens: float32 [8, 1024, 768], P('expert', 'shard')
- grad_gain_attn: float32 [768], P('shard')
- grad_pos_table: float32 [32, 12], P('shard')
- grad_w_query: float32 [768, 768], P('shard')
- grad_w_key: float32 [768, 768], P('shard')
- grad_w_value: float32 [768, 768], P('shard')
- grad_w_attn_out: float32 [768, 768], P('shard')
- grad_w_router: float32 [768, 8], P('shard')
- grad_gain_ffn: float32 [768], P('shard')
- grad_w_in: float32 [8, 768, 3072], P('expert', None, 'shard')
- grad_w_out: float32 [8, 3072, 768], P('expert', 'shard')
Inputs may be any that keep to these rules, and one draw needn't show every extreme that they name: `expert_ids`: one expert, drawn from the seed, is chosen by 4 or more tokens in every aligned block of 256 tokens of a sequence. For a kept token, slots counts the earlier tokens of its aligned block of 256 tokens that chose the same expert; for a dropped token it is 3. keep is 1 exactly for the first 4 tokens of each aligned block of 256 tokens that choose a given expert, so the kept tokens of a block and expert have distinct slots, and in every block some expert has 4 kept tokens.
All inputs are finite; a program needn't handle non-finite values.
Results may differ from a plain program's by a relative error of at most 0.02.
Values may be sent and summed in bfloat16 or wider, within the bound.
No kernel may reach another device: no remote copies, remote signals or barrier semaphores. Data moves between devices by JAX's collectives and lax.ppermute only.
A program may use at most 320 MiB of HBM per device.

v0:
```python
import jax
import jax.numpy as jnp
from jax import lax
from jax.sharding import PartitionSpec as P

HEADS = 12
HEAD_DIM = 64
CAP = 4


best_expert = lax.Precision.HIGHEST
epsilon = 1e-06
contract_first = (((0,), (0,)), ((), ()))


def rms_factor(values):
    return lax.rsqrt(jnp.mean(values * values, axis=-1, keepdims=True) + epsilon)


def norm_back(grad_normed, normed_pre, factor):
    return factor * (
        grad_normed - normed_pre * jnp.mean(grad_normed * normed_pre, axis=-1, keepdims=True)
    )


def gelu_back(hidden, grad_act):
    return jax.vjp(jax.nn.gelu, hidden)[1](grad_act)[0]


def diagonal_sums(score_grads):
    head_count, row_count, col_count = score_grads.shape
    padded = jnp.pad(score_grads, ((0, 0), (0, 0), (row_count, 0)))
    flattened = padded.reshape(head_count, row_count * (col_count + row_count))
    flattened = jnp.pad(flattened, ((0, 0), (0, row_count)))
    skewed = flattened.reshape(head_count, row_count, col_count + row_count + 1)
    return jnp.sum(skewed, axis=1, dtype=jnp.float32)[:, 1:-1]


def offset_table(table_full, buckets, block_rows, total_rows):
    first_row = total_rows - block_rows - lax.axis_index("shard") * block_rows
    window = lax.dynamic_slice_in_dim(buckets, first_row, total_rows + block_rows - 1)
    onehot = (window[:, None] == jnp.arange(table_full.shape[0])[None, :]).astype(jnp.float32)
    per_offset = jnp.dot(onehot, table_full.astype(jnp.float32), precision=best_expert)
    return (onehot, per_offset.T)


def score_grid(queries, keys_all, per_offset, block_rows, total_rows):
    q_heads = queries.reshape(block_rows, HEADS, HEAD_DIM)
    key_head_rows = keys_all.reshape(total_rows, HEADS, HEAD_DIM)
    offset_index = (
        jnp.arange(total_rows)[None, :] - jnp.arange(block_rows)[:, None] + block_rows - 1
    )
    offset_bias = per_offset[:, offset_index]
    return (
        jnp.einsum("ihd,jhd->hij", q_heads, key_head_rows, preferred_element_type=jnp.float32)
        * HEAD_DIM ** (-0.5)
        + offset_bias
    )


def per_device(
    tokens,
    gain_attn,
    pos_table,
    buckets,
    w_query,
    w_key,
    w_value,
    w_attn_out,
    w_router,
    gain_ffn,
    w_in,
    w_out,
    expert_ids,
    slots,
    keep,
    grad_out,
):
    gain_one, table_full, query_w, key_w, value_w, out_w, router_weight, gain_two = (
        lax.all_gather(gain_attn, "shard", axis=0, tiled=True),
        lax.all_gather(pos_table, "shard", axis=0, tiled=True),
        lax.all_gather(w_query, "shard", axis=0, tiled=True),
        lax.all_gather(w_key, "shard", axis=0, tiled=True),
        lax.all_gather(w_value, "shard", axis=0, tiled=True),
        lax.all_gather(w_attn_out, "shard", axis=0, tiled=True),
        lax.all_gather(w_router, "shard", axis=0, tiled=True),
        lax.all_gather(gain_ffn, "shard", axis=0, tiled=True),
    )
    block_rows = tokens.shape[1]
    model_width = tokens.shape[2]
    total_rows = block_rows * lax.axis_size("shard")
    tokens_f = tokens[0].astype(jnp.float32)
    factor_one = rms_factor(tokens_f)
    normed_pre = tokens_f * factor_one
    gain_one_f = gain_one.astype(jnp.float32)
    normed = (normed_pre * gain_one_f).astype(jnp.bfloat16)
    queries = jnp.dot(normed, query_w, preferred_element_type=jnp.float32).astype(jnp.bfloat16)
    keys = jnp.dot(normed, key_w, preferred_element_type=jnp.float32).astype(jnp.bfloat16)
    values = jnp.dot(normed, value_w, preferred_element_type=jnp.float32).astype(jnp.bfloat16)
    keys_all, values_all = (
        lax.all_gather(keys, "shard", axis=0, tiled=True),
        lax.all_gather(values, "shard", axis=0, tiled=True),
    )
    onehot_pos, per_offset = offset_table(table_full, buckets, block_rows, total_rows)
    scores = score_grid(queries, keys_all, per_offset, block_rows, total_rows)
    row_peak = jnp.max(scores, axis=-1, keepdims=True)
    row_total = jnp.sum(jnp.exp(scores - row_peak), axis=-1, keepdims=True)
    log_total = row_peak + jnp.log(row_total)
    probs_low = (jnp.exp(scores - row_peak) / row_total).astype(jnp.bfloat16)
    v_heads = values_all.reshape(total_rows, HEADS, HEAD_DIM)
    mixed_heads = (
        jnp.einsum("hij,jhd->ihd", probs_low, v_heads, preferred_element_type=jnp.float32)
        .reshape(block_rows, model_width)
        .astype(jnp.bfloat16)
    )
    residual = tokens_f + jnp.dot(mixed_heads, out_w, preferred_element_type=jnp.float32)
    factor_two = rms_factor(residual)
    normed_two_pre = residual * factor_two
    gain_two_f = gain_two.astype(jnp.float32)
    feedforward_input = (normed_two_pre * gain_two_f).astype(jnp.bfloat16)
    router_scores = jnp.dot(feedforward_input, router_weight, preferred_element_type=jnp.float32)
    expert_count = router_weight.shape[1]
    router_probs = jax.nn.softmax(router_scores, axis=-1)
    chosen = (expert_ids[0][:, None] == jnp.arange(expert_count)[None, :]).astype(jnp.float32)
    gating = jnp.sum(router_probs * chosen, axis=-1)
    target_slot = expert_ids[0] * CAP + slots[0]
    placing = (
        (target_slot[None, :] == jnp.arange(expert_count * CAP)[:, None]) & (keep[0][None, :] > 0)
    ).astype(jnp.bfloat16)
    outgoing = (
        jnp.dot(placing, feedforward_input, preferred_element_type=jnp.float32)
        .astype(jnp.bfloat16)
        .reshape(expert_count, CAP, model_width)
    )
    arrived = lax.all_to_all(outgoing, "expert", split_axis=0, concat_axis=0, tiled=True)
    arrived_rows = arrived.reshape(-1, model_width)
    first_part = w_in[0]
    second_part = w_out[0]
    rows_all = lax.all_gather(arrived_rows, "shard", axis=0, tiled=True)
    hidden = jnp.dot(rows_all, first_part, preferred_element_type=jnp.float32)
    activation = jax.nn.gelu(hidden).astype(jnp.bfloat16)
    partial_out = jnp.dot(activation, second_part, preferred_element_type=jnp.float32)
    expert_out = lax.psum_scatter(partial_out, "shard", scatter_dimension=0, tiled=True).astype(
        jnp.bfloat16
    )
    returned = lax.all_to_all(
        expert_out.reshape(-1, CAP, model_width), "expert", split_axis=0, concat_axis=0, tiled=True
    )
    token_out = lax.dot_general(
        placing,
        returned.reshape(-1, model_width),
        contract_first,
        preferred_element_type=jnp.float32,
    )
    output = (residual + gating[:, None] * token_out).astype(jnp.bfloat16)
    grad_y = grad_out[0].astype(jnp.float32)
    grad_gate = jnp.sum(grad_y * token_out, axis=-1)
    placing_f = placing.astype(jnp.float32)
    slot_grads = jnp.dot(placing_f, gating[:, None] * grad_y, precision=best_expert).astype(
        jnp.bfloat16
    )
    grad_back = lax.all_to_all(
        slot_grads.reshape(expert_count, CAP, model_width),
        "expert",
        split_axis=0,
        concat_axis=0,
        tiled=True,
    )
    local_gradient = grad_back.reshape(-1, model_width)
    grad_rows_all = lax.all_gather(local_gradient, "shard", axis=0, tiled=True)
    grad_act = jnp.dot(grad_rows_all, second_part.T, preferred_element_type=jnp.float32)
    grad_hidden = gelu_back(hidden, grad_act).astype(jnp.bfloat16)
    grad_second = jnp.dot(activation.T, grad_rows_all, preferred_element_type=jnp.float32)
    grad_first = jnp.dot(rows_all.T, grad_hidden, preferred_element_type=jnp.float32)
    grad_partial = jnp.dot(grad_hidden, first_part.T, preferred_element_type=jnp.float32)
    grad_rows = lax.psum_scatter(grad_partial, "shard", scatter_dimension=0, tiled=True).astype(
        jnp.bfloat16
    )
    sent_gradient = lax.all_to_all(
        grad_rows.reshape(-1, CAP, model_width), "expert", split_axis=0, concat_axis=0, tiled=True
    )
    grad_ffn_expert = lax.dot_general(
        placing,
        sent_gradient.reshape(-1, model_width),
        contract_first,
        preferred_element_type=jnp.float32,
    )
    grad_logits = (grad_gate * gating)[:, None] * (chosen - router_probs)
    grad_router = jnp.dot(
        feedforward_input.astype(jnp.float32).T, grad_logits, precision=best_expert
    )
    grad_ffn = grad_ffn_expert + jnp.dot(
        grad_logits, router_weight.astype(jnp.float32).T, precision=best_expert
    )
    grad_gain_two = jnp.sum(grad_ffn * normed_two_pre, axis=0)
    grad_residual = grad_y + norm_back(grad_ffn * gain_two_f, normed_two_pre, factor_two)
    grad_att = grad_residual.astype(jnp.bfloat16)
    grad_out_w = jnp.dot(mixed_heads.T, grad_att, preferred_element_type=jnp.float32)
    grad_mixed = (
        jnp.dot(grad_att, out_w.T, preferred_element_type=jnp.float32)
        .astype(jnp.bfloat16)
        .reshape(block_rows, HEADS, HEAD_DIM)
    )
    scores_again = score_grid(queries, keys_all, per_offset, block_rows, total_rows)
    probs = jnp.exp(scores_again - log_total)
    grad_probs = jnp.einsum("ihd,jhd->hij", grad_mixed, v_heads, preferred_element_type=jnp.float32)
    grad_scores = (
        probs * (grad_probs - jnp.sum(probs * grad_probs, axis=-1, keepdims=True))
    ).astype(jnp.bfloat16)
    offset_grads = diagonal_sums(grad_scores)
    grad_table = jnp.dot(onehot_pos.T, offset_grads.T, precision=best_expert)
    q_heads = queries.reshape(block_rows, HEADS, HEAD_DIM)
    key_head_rows = keys_all.reshape(total_rows, HEADS, HEAD_DIM)
    score_scale = HEAD_DIM ** (-0.5)
    grad_queries = (
        (
            jnp.einsum(
                "hij,jhd->ihd", grad_scores, key_head_rows, preferred_element_type=jnp.float32
            )
            * score_scale
        )
        .reshape(block_rows, model_width)
        .astype(jnp.bfloat16)
    )
    keys_partial = (
        jnp.einsum(
            "hij,ihd->jhd", grad_scores, q_heads, preferred_element_type=jnp.float32
        ).reshape(total_rows, model_width)
        * score_scale
    )
    values_partial = jnp.einsum(
        "hij,ihd->jhd", probs_low, grad_mixed, preferred_element_type=jnp.float32
    ).reshape(total_rows, model_width)
    grad_keys, grad_values = (
        lax.psum_scatter(
            keys_partial.astype(jnp.bfloat16), "shard", scatter_dimension=0, tiled=True
        ).astype(jnp.float32),
        lax.psum_scatter(
            values_partial.astype(jnp.bfloat16), "shard", scatter_dimension=0, tiled=True
        ).astype(jnp.float32),
    )
    grad_keys = grad_keys.astype(jnp.bfloat16)
    grad_values = grad_values.astype(jnp.bfloat16)
    grad_query_w = jnp.dot(normed.T, grad_queries, preferred_element_type=jnp.float32)
    grad_key_w = jnp.dot(normed.T, grad_keys, preferred_element_type=jnp.float32)
    grad_value_w = jnp.dot(normed.T, grad_values, preferred_element_type=jnp.float32)
    grad_normed = jnp.dot(grad_queries, query_w.T, preferred_element_type=jnp.float32)
    grad_normed = grad_normed + jnp.dot(grad_keys, key_w.T, preferred_element_type=jnp.float32)
    grad_normed = grad_normed + jnp.dot(grad_values, value_w.T, preferred_element_type=jnp.float32)
    grad_gain_one = jnp.sum(grad_normed * normed_pre, axis=0)
    grad_tokens = grad_residual + norm_back(grad_normed * gain_one_f, normed_pre, factor_one)
    part_one, part_table, part_query, part_key, part_value, part_out, part_router, part_two = (
        lax.psum_scatter(
            grad_gain_one.astype(jnp.bfloat16), "shard", scatter_dimension=0, tiled=True
        ).astype(jnp.float32),
        lax.psum_scatter(
            grad_table.astype(jnp.bfloat16), "shard", scatter_dimension=0, tiled=True
        ).astype(jnp.float32),
        lax.psum_scatter(
            grad_query_w.astype(jnp.bfloat16), "shard", scatter_dimension=0, tiled=True
        ).astype(jnp.float32),
        lax.psum_scatter(
            grad_key_w.astype(jnp.bfloat16), "shard", scatter_dimension=0, tiled=True
        ).astype(jnp.float32),
        lax.psum_scatter(
            grad_value_w.astype(jnp.bfloat16), "shard", scatter_dimension=0, tiled=True
        ).astype(jnp.float32),
        lax.psum_scatter(
            grad_out_w.astype(jnp.bfloat16), "shard", scatter_dimension=0, tiled=True
        ).astype(jnp.float32),
        lax.psum_scatter(
            grad_router.astype(jnp.bfloat16), "shard", scatter_dimension=0, tiled=True
        ).astype(jnp.float32),
        lax.psum_scatter(
            grad_gain_two.astype(jnp.bfloat16), "shard", scatter_dimension=0, tiled=True
        ).astype(jnp.float32),
    )
    (
        total_one,
        total_table,
        total_query,
        total_key,
        total_value,
        total_out,
        total_router,
        total_two,
    ) = lax.psum(
        (part_one, part_table, part_query, part_key, part_value, part_out, part_router, part_two),
        "expert",
    )
    return (
        output[None],
        grad_tokens[None],
        total_one,
        total_table,
        total_query,
        total_key,
        total_value,
        total_out,
        total_router,
        total_two,
        grad_first[None],
        grad_second[None],
    )


def solution(mesh):
    in_specs = (
        P("expert", "shard", None),
        P("shard"),
        P("shard", None),
        P(),
        P("shard", None),
        P("shard", None),
        P("shard", None),
        P("shard", None),
        P("shard", None),
        P("shard"),
        P("expert", None, "shard"),
        P("expert", "shard", None),
        P("expert", "shard"),
        P("expert", "shard"),
        P("expert", "shard"),
        P("expert", "shard", None),
    )
    out_specs = (
        P("expert", "shard", None),
        P("expert", "shard", None),
        P("shard"),
        P("shard", None),
        P("shard", None),
        P("shard", None),
        P("shard", None),
        P("shard", None),
        P("shard", None),
        P("shard"),
        P("expert", None, "shard"),
        P("expert", "shard", None),
    )
    return jax.shard_map(
        per_device, mesh=mesh, in_specs=in_specs, out_specs=out_specs, check_vma=False
    )
```

profile of v0, /device:TPU:0, one launch (start us, length us, event | category | flops | bytes accessed | tf_op | source)
XLA Modules:
  0.0 1459.3 jit_solution(5047390003031893377)
XLA Ops:
  13.2 8.3 all-reduce.9
  22.6 7.1 all-gather.14.cloned.1.call-done
  32.5 16.3 %all-gather.8.cloned.1.call-done = bf16[768,768]{1,0:T(8,128)(2,1)} async-done(((bf16[192,768]{1,0:T(8,128)(2,1)}), bf16[768,768]{1,0:T(8,128)(2,1)}) %all-gather.8.cloned.1.call-update) | async-done | bytes 1179664 | tf_op jit(solution)/shard_map/all_gather | solution.py:84
  58.4 865.8 %gather_fusion = f32[262144,12]{1,0:T(8,128)} fusion(f32[12,1279]{0,1:T(8,128)S(1)} %copy.48, s32[262144]{0:T(1024)S(1)} %broadcast_clamp_fusion), kind=kCustom, calls=%fused_computation | custom fusion | bytes 26214400 | tf_op jit(solution)/shard_map/gather | solution.py:53
  924.2 76.0 %copy.52 = f32[256,1024,12]{1,0,2:T(8,128)} copy(f32[256,1024,12]{2,1,0:T(8,128)} %bitcast.6) | data formatting | bytes 25165824 | tf_op jit(solution)/shard_map/gather | solution.py:53
  1000.2 5.2 all-gather
  1010.1 6.2 fusion.80
  1026.1 6.6 divide_convert_fusion
  1040.9 5.5 all-to-all-start
  1056.7 5.6 all_gather.46
  1063.3 5.8 all_gather.47
  1076.1 17.7 %reduce-scatter.14.cloned.1.call-done = f32[32,768]{1,0:T(8,128)} async-done(((f32[128,768]{1,0:T(8,128)}), f32[32,768]{1,0:T(8,128)}) %reduce-scatter.14.cloned.1.call-update) | async-done | bytes 98320 | tf_op jit(solution)/shard_map/reduce_scatter | solution.py:176
  1095.4 5.5 all-to-all-start.3
  1100.9 16.9 %reduce-scatter.12.cloned.1.call-done = f32[32,768]{1,0:T(8,128)} async-done(((f32[128,768]{1,0:T(8,128)}), f32[32,768]{1,0:T(8,128)}) %reduce-scatter.12.cloned.1.call-update) | async-done | bytes 98320 | tf_op jit(solution)/shard_map/reduce_scatter | solution.py:143
  1119.3 5.5 all-to-all-start.1
  1125.2 6.4 all-to-all-done.1
  1137.7 11.2 multiply_reduce_fusion
  1150.7 6.2 multiply_convert_fusion
  1160.1 5.4 convolution_convert_fusion
  1166.7 5.3 fusion.1
  1175.5 9.5 reduce-scatter.16.cloned.1.call-done
  1193.2 7.0 pad.8
  1200.2 8.1 pad.11
  1208.3 13.9 copy.56
  1224.9 11.8 pad_convert_fusion
  1236.7 31.8 %reshape.188 = f32[12,256,1281]{2,1,0:T(8,128)} reshape(f32[12,327936]{1,0:T(8,128)} %pad_convert_fusion) | data formatting | bytes 31481856 | tf_op jit(solution)/shard_map/convert_element_type | solution.py:36
  1268.5 6.9 reduce_sum.118
  1279.0 16.1 %reduce-scatter.26.cloned.1.call-done = bf16[192,768]{1,0:T(8,128)(2,1)} async-done(((bf16[768,768]{1,0:T(8,128)(2,1)}), bf16[192,768]{1,0:T(8,128)(2,1)}) %reduce-scatter.26.cloned.1.call-update) | async-done | bytes 294928 | tf_op jit(solution)/shard_map/reduce_scatter | solution.py:268
  1298.5 10.1 all-reduce.8
  1311.0 12.3 reduce-scatter.22.cloned.1.call-done
  1323.3 28.3 %reduce-scatter.24.cloned.1.call-done = bf16[192,768]{1,0:T(8,128)(2,1)} async-done(((bf16[768,768]{1,0:T(8,128)(2,1)}), bf16[192,768]{1,0:T(8,128)(2,1)}) %reduce-scatter.24.cloned.1.call-update) | async-done | bytes 294928 | tf_op jit(solution)/shard_map/reduce_scatter | solution.py:265
  1351.6 100.9 %all-reduce.11 = (f32[192]{0:T(256)}, f32[8,12]{1,0:T(8,128)}, f32[192,768]{1,0:T(8,128)}, f32[192,768]{1,0:T(8,128)}, f32[192,768]{1,0:T(8,128)}, /*index=5*/f3...) all-reduce(f32[192]{0:T(256)S(1)} %get-tuple-element.46, ...), channel_id=1, replica_groups=mesh['expert'=8,'shard'=4] {'expert'}, use_global_device_ids=true, to_apply=%region_17.18 | all-reduce | flops 591840 | bytes 3552000 | tf_op jit(solution)/shard_map/psum | solution.py:287
  (195 shorter events, 97.3 us)
Async XLA Ops:
  7.2 1061.9 %copy-start = (bf16[1,768,768]{2,1,0:T(8,128)(2,1)S(1)}, bf16[1,768,768]{2,1,0:T(8,128)(2,1)}, u32[]{:S(2)}) copy-start(bf16[1,768,768]{2,1,0:T(8,128)(2,1)} %param.26) | copy-start | bytes 3538948
  7.2 22.6 %all-gather.14.cloned.1.call-start = ((), (), s32[]{:S(2)}) async-start(), calls=%async_computation.16 | async-start | bytes 1474560 | tf_op jit(solution)/shard_map/all_gather | solution.py:83
  7.9 40.9 %all-gather.8.cloned.1.call-start = ((), (), s32[]{:S(2)}) async-start(), calls=%async_computation.13 | async-start | bytes 1474560 | tf_op jit(solution)/shard_map/all_gather | solution.py:84
  8.7 996.9 %all-gather.12.cloned.1.call-start = ((), (), s32[]{:S(2)}) async-start(), calls=%async_computation.15 | async-start | bytes 1474560 | tf_op jit(solution)/shard_map/all_gather | solution.py:82
  9.4 998.1 %all-gather.16.cloned.1.call-start = ((), (), s32[]{:S(2)}) async-start(), calls=%async_computation.17 | async-start | bytes 1966080 | tf_op jit(solution)/shard_map/all_gather | solution.py:101
  32.5 991.0 %all-gather.10.cloned.1.call-start = ((), (), s32[]{:S(2)}) async-start(), calls=%async_computation.14 | async-start | bytes 1966080 | tf_op jit(solution)/shard_map/all_gather | solution.py:102
  51.4 986.0 %all-gather.18.cloned.1.call-start = ((), (), s32[]{:S(2)}) async-start(), calls=%async_computation.18 | async-start | bytes 1474560 | tf_op jit(solution)/shard_map/all_gather | solution.py:85
  924.2 76.0 %copy-start.34 = (s32[1,256]{1,0:T(1,128)S(1)}, s32[1,256]{1,0:T(1,128)}, u32[]{:S(2)}) copy-start(s32[1,256]{1,0:T(1,128)} %param.30) | copy-start | bytes 3076
  924.2 76.1 %copy-start.31 = (bf16[192,8]{0,1:T(8,128)(2,1)S(1)}, bf16[192,8]{0,1:T(8,128)(2,1)}, u32[]{:S(2)}) copy-start(bf16[192,8]{0,1:T(8,128)(2,1)} %param.24) | copy-start | bytes 9220
  924.2 81.4 %copy-start.23 = (s32[1,256]{1,0:T(1,128)S(1)}, s32[1,256]{1,0:T(1,128)}, u32[]{:S(2)}) copy-start(s32[1,256]{1,0:T(1,128)} %param.28) | copy-start | bytes 3076
  924.2 81.4 %copy-start.33 = (s32[1,256]{1,0:T(1,128)S(1)}, s32[1,256]{1,0:T(1,128)}, u32[]{:S(2)}) copy-start(s32[1,256]{1,0:T(1,128)} %param.29) | copy-start | bytes 3076
  1000.2 46.5 %copy-start.29 = (pred[256]{0:T(512)(128)(4,1)}, pred[256]{0:T(512)(128)(4,1)S(1)}, u32[]{:S(2)}) copy-start(pred[256]{0:T(512)(128)(4,1)S(1)} %compare_reduce_fusion) | copy-start | bytes 772
  1039.4 92.6 %copy-start.7 = (f32[256,768]{1,0:T(8,128)}, f32[256,768]{1,0:T(8,128)S(1)}, u32[]{:S(2)}) copy-start(f32[256,768]{1,0:T(8,128)S(1)} %get-tuple-element.36) | copy-start | bytes 2359300
  1040.9 12.3 all-to-all-start
  1053.2 10.1 all-to-all-start.2
  1056.6 37.2 %reduce-scatter.14.cloned.1.call-start = ((), (), s32[]{:S(2)}) async-start(), calls=%async_computation.20 | async-start | bytes 491520 | tf_op jit(solution)/shard_map/reduce_scatter | solution.py:176
  1072.2 52.7 %copy-start.30 = (pred[256]{0:T(512)(128)(4,1)S(1)}, pred[256]{0:T(512)(128)(4,1)}, u32[]{:S(2)}) copy-start(pred[256]{0:T(512)(128)(4,1)} %copy-done.29) | copy-start | bytes 772
  1073.5 58.1 %copy-start.11 = (bf16[1,256,768]{2,1,0:T(8,128)(2,1)S(1)}, bf16[1,256,768]{2,1,0:T(8,128)(2,1)}, u32[]{:S(2)}) copy-start(bf16[1,256,768]{2,1,0:T(8,128)(2,1)} %param.31) | copy-start | bytes 1179652
  1073.5 58.5 %copy-start.25 = (f32[256]{0:T(256)S(1)}, f32[256]{0:T(256)}, u32[]{:S(2)}) copy-start(f32[256]{0:T(256)} %copy-done.24) | copy-start | bytes 3076
  1073.5 44.2 %reduce-scatter.12.cloned.1.call-start = ((), (), s32[]{:S(2)}) async-start(), calls=%async_computation.19 | async-start | bytes 491520 | tf_op jit(solution)/shard_map/reduce_scatter | solution.py:143
  1095.4 23.9 %all-to-all-start.3 = ((bf16[8,4,768]{2,1,0:T(4,128)(2,1)}), bf16[8,4,768]{2,1,0:T(4,128)(2,1)S(1)}, u32[]{:S(2)}, u32[]{:S(2)}) async-start(bf16[8,4,768]{2,1,0:T(4,128)(2,1)} %reshape.182), calls=%async_computation.5 | async-start | bytes 98304 | tf_op jit(solution)/shard_map/all_to_all | solution.py:179
  1119.3 12.3 all-to-all-start.1
  1124.8 60.2 %reduce-scatter.16.cloned.1.call-start = ((), (), s32[]{:S(2)}) async-start(), calls=%async_computation.21 | async-start | bytes 1966080 | tf_op jit(solution)/shard_map/reduce_scatter | solution.py:235
  1160.1 62.1 %reduce-scatter.18.cloned.1.call-start = ((), (), s32[]{:S(2)}) async-start(), calls=%async_computation.22 | async-start | bytes 1966080 | tf_op jit(solution)/shard_map/reduce_scatter | solution.py:238
  1165.6 112.6 %reduce-scatter.28.cloned.1.call-start = ((), (), s32[]{:S(2)}) async-start(), calls=%async_computation.27 | async-start | bytes 245760
  1172.1 106.9 %reduce-scatter.20.cloned.1.call-start = ((), (), s32[]{:S(2)}) async-start(), calls=%async_computation.23 | async-start | bytes 1474560 | tf_op jit(solution)/shard_map/reduce_scatter | solution.py:259
  1173.8 121.3 %reduce-scatter.26.cloned.1.call-start = ((), (), s32[]{:S(2)}) async-start(), calls=%async_computation.26 | async-start | bytes 1474560 | tf_op jit(solution)/shard_map/reduce_scatter | solution.py:268
  1175.4 147.8 %reduce-scatter.22.cloned.1.call-start = ((), (), s32[]{:S(2)}) async-start(), calls=%async_computation.24 | async-start | bytes 1474560 | tf_op jit(solution)/shard_map/reduce_scatter | solution.py:262
  1187.6 164.0 %reduce-scatter.24.cloned.1.call-start = ((), (), s32[]{:S(2)}) async-start(), calls=%async_computation.25 | async-start | bytes 1474560 | tf_op jit(solution)/shard_map/reduce_scatter | solution.py:265
  1297.0 54.6 %copy-start.21 = (bf16[192,768]{1,0:T(8,128)(2,1)S(1)}, bf16[192,768]{1,0:T(8,128)(2,1)}, u32[]{:S(2)}) copy-start(bf16[192,768]{1,0:T(8,128)(2,1)} %reduce-scatter.20.cloned.1.call-done) | copy-start | bytes 884740
  1297.0 54.6 %copy-start.22 = (bf16[192,768]{1,0:T(8,128)(2,1)S(1)}, bf16[192,768]{1,0:T(8,128)(2,1)}, u32[]{:S(2)}) copy-start(bf16[192,768]{1,0:T(8,128)(2,1)} %reduce-scatter.26.cloned.1.call-done) | copy-start | bytes 884740
  1297.1 155.5 %copy-start.1 = (bf16[1,768,768]{2,1,0:T(8,128)(2,1)S(1)}, bf16[1,768,768]{2,1,0:T(8,128)(2,1)}, u32[]{:S(2)}) copy-start(bf16[1,768,768]{2,1,0:T(8,128)(2,1)} %param.26) | copy-start | bytes 3538948
  (25 other events, 225.0 us)
Sparse Core Ops, SparseCore 0:
  9.6 20.1 all-gather.13
  31.3 17.4 all-gather.7
  50.4 17.4 all-gather.11
  69.9 19.6 all-gather.15
  91.6 19.6 all-gather.9
  112.7 17.4 all-gather.17
  1073.6 20.1 reduce-scatter.13
  1096.9 20.7 reduce-scatter.11
  1160.2 24.6 reduce-scatter.15
  1187.5 28.1 reduce-scatter.17
  1218.7 19.7 reduce-scatter.27
  1240.9 25.7 reduce-scatter.19
  1269.4 25.7 reduce-scatter.25
  1297.5 25.7 reduce-scatter.21
  1325.9 25.7 reduce-scatter.23
where the time goes:
time: 1470 us; the launch traced here: 1460 us
  local copies, waits for them, and re-layouts  1030 us (70%)
  blocking collectives  141 us (10%)
  waiting for transfers between devices  139 us (9%)
  matrix products  71.8 us (5%)
  other arithmetic  42.3 us (3%)
  starting transfers between devices  20.9 us (1%)
  between operations  16.7 us (1%)
    gather x2, local copies, waits for them, and re-layouts, score_grid(): offset_bias = per_offset[:, offset_index]  942 us
    psum x1, blocking collectives, per_device(): lax.psum((part_one, part_table, part_query, part_key, part_value, part_ou...  101 us
    unnamed x87, local copies, waits for them, and re-layouts  37.6 us
    convert_element_type x1, local copies, waits for them, and re-layouts, diagonal_sums(): return jnp.sum(skewed, axis=1, dtype=jnp.float32)[:, 1:-1]  31.8 us
  transfers between devices with their start and end apart: 19, of which 11 were waited for; matrix products, arithmetic and copies ran while one was open for 75% of the time, Pallas kernels for 0%

commit v1 on v0

v1 whole, which is shorter than its diff:
```python
import functools

import jax
import jax.numpy as jnp
from jax import lax
from jax.experimental import pallas as pl
from jax.experimental.pallas import tpu as pltpu
from jax.sharding import PartitionSpec as P

HEADS = 12
HEAD_DIM = 64
CAP = 4
QBLOCK = 256

bf16 = jnp.bfloat16
f32 = jnp.float32
highest = lax.Precision.HIGHEST
epsilon = 1e-06
score_scale = HEAD_DIM ** (-0.5)

NN = (((1,), (0,)), ((), ()))
NT = (((1,), (1,)), ((), ()))
TN = (((0,), (0,)), ((), ()))


def mm(a, b, dims=NN):
    return lax.dot_general(a, b, dims, preferred_element_type=f32)


def mm_exact(a, b, dims=NN):
    return lax.dot_general(a, b, dims, precision=highest, preferred_element_type=f32)


def rms_factor(values):
    return lax.rsqrt(jnp.mean(values * values, axis=-1, keepdims=True) + epsilon)


def norm_back(grad_normed, normed_pre, factor):
    return factor * (
        grad_normed - normed_pre * jnp.mean(grad_normed * normed_pre, axis=-1, keepdims=True)
    )


def gelu_back(hidden, grad_act):
    return jax.vjp(jax.nn.gelu, hidden)[1](grad_act)[0]


def swap(value, axis, bits):
    count = lax.axis_size(axis)
    return lax.ppermute(value, axis, [(i, i ^ bits) for i in range(count)])


def partner(axis, bits):
    return jnp.bitwise_xor(lax.axis_index(axis), bits)


def take(stacked, index):
    return lax.dynamic_index_in_dim(stacked, index, axis=0, keepdims=False)


def gather_pairs(value, axis):
    count = lax.axis_size(axis)
    held = value[None]
    step = count // 2
    order = [0]
    while step >= 1:
        held = jnp.concatenate([held, swap(held, axis, step)], axis=0)
        order = order + [o ^ step for o in order]
        step //= 2
    return [held[order.index(t)] for t in range(count)]


def in_order(blocks, axis):
    out = jnp.zeros((len(blocks),) + blocks[0].shape, blocks[0].dtype)
    for t, block in enumerate(blocks):
        out = lax.dynamic_update_slice_in_dim(out, block[None], partner(axis, t), axis=0)
    return out


def bias_rows(offsets_row, width):
    rows = jnp.broadcast_to(offsets_row, (8, width))
    rows = pltpu.roll(rows, width - (QBLOCK - 1), 1)
    place = lax.broadcasted_iota(jnp.int32, (8, width), 0)
    for bit in (1, 2, 4):
        rows = jnp.where((place & bit) != 0, pltpu.roll(rows, bit, 1), rows)
    count = 8
    while count < QBLOCK:
        rows = jnp.concatenate([rows, pltpu.roll(rows, count, 1)], axis=0)
        count *= 2
    return rows


def diagonal_row(grid, width):
    count = QBLOCK
    while count > 8:
        count //= 2
        grid = grid[:count] + pltpu.roll(grid[count:], width - count, 1)
    place = lax.broadcasted_iota(jnp.int32, (8, width), 0)
    for bit in (4, 2, 1):
        grid = jnp.where((place & bit) != 0, pltpu.roll(grid, width - bit, 1), grid)
    return pltpu.roll(jnp.sum(grid, axis=0, keepdims=True), QBLOCK - 1, 1)


def attention_forward_kernel(q_ref, k_ref, v_ref, table_ref, onehot_ref, mixed_ref, log_ref, bias_ref):
    total = q_ref.shape[0]
    width = onehot_ref.shape[1]
    heads = q_ref.shape[1] // HEAD_DIM
    blocks = total // QBLOCK
    offsets = mm(table_ref[...], onehot_ref[...])
    for h in range(heads):
        cols = slice(h * HEAD_DIM, (h + 1) * HEAD_DIM)
        bias_ref[...] = bias_rows(offsets[h : h + 1, :], width)
        keys = k_ref[:, cols]
        values = v_ref[:, cols]
        for a in range(blocks):
            rows = slice(a * QBLOCK, (a + 1) * QBLOCK)
            start = total - QBLOCK * (a + 1)
            scores = mm(q_ref[rows, cols], keys, NT) * score_scale
            scores = scores + bias_ref[:, start : start + total]
            peak = jnp.max(scores, axis=-1, keepdims=True)
            raised = jnp.exp(scores - peak)
            norm = jnp.sum(raised, axis=-1, keepdims=True)
            probs_low = (raised * (1.0 / norm)).astype(bf16)
            mixed_ref[rows, cols] = mm(probs_low, values).astype(bf16)
            log_ref[rows, h : h + 1] = peak + jnp.log(norm)


def attention_backward_kernel(
    q_ref, k_ref, v_ref, gm_ref, log_ref, table_ref, onehot_ref,
    gq_ref, gk_ref, gv_ref, gt_ref, bias_ref, sums_ref, diag_ref,
):
    total = q_ref.shape[0]
    width = onehot_ref.shape[1]
    heads = q_ref.shape[1] // HEAD_DIM
    blocks = total // QBLOCK
    offsets = mm(table_ref[...], onehot_ref[...])
    diag_ref[...] = jnp.zeros_like(diag_ref)
    for h in range(heads):
        cols = slice(h * HEAD_DIM, (h + 1) * HEAD_DIM)
        bias_ref[...] = bias_rows(offsets[h : h + 1, :], width)
        sums_ref[...] = jnp.zeros_like(sums_ref)
        keys = k_ref[:, cols]
        values = v_ref[:, cols]
        gk = jnp.zeros((HEAD_DIM, total), f32)
        gv = jnp.zeros((HEAD_DIM, total), f32)
        for a in range(blocks):
            rows = slice(a * QBLOCK, (a + 1) * QBLOCK)
            start = total - QBLOCK * (a + 1)
            queries = q_ref[rows, cols]
            gm = gm_ref[rows, cols]
            scores = mm(queries, keys, NT) * score_scale
            scores = scores + bias_ref[:, start : start + total]
            probs = jnp.exp(scores - log_ref[rows, h : h + 1])
            grad_probs = mm(gm, values, NT)
            dots = jnp.sum(probs * grad_probs, axis=-1, keepdims=True)
            grad_scores_f = probs * (grad_probs - dots)
            grad_scores = grad_scores_f.astype(bf16)
            sums_ref[:, start : start + total] += grad_scores.astype(f32)
            gq_ref[rows, cols] = (mm(grad_scores, keys) * score_scale).astype(bf16)
            gk = gk + mm(queries, grad_scores, TN)
            gv = gv + mm(gm, probs.astype(bf16), TN)
        gk_ref[:, cols] = (gk * score_scale).T.astype(bf16)
        gv_ref[:, cols] = gv.T.astype(bf16)
        diag_ref[h : h + 1, :] = diagonal_row(sums_ref[...], width)
    gt_ref[...] = mm_exact(diag_ref[...], onehot_ref[...].astype(f32), NT)


def vmem_specs(count):
    return [pl.BlockSpec(memory_space=pltpu.VMEM)] * count


def attention_forward(queries, keys, values, table, onehot):
    total, width = queries.shape
    flops = 4 * total * total * width
    return pl.pallas_call(
        attention_forward_kernel,
        out_shape=(
            jax.ShapeDtypeStruct((total, width), bf16),
            jax.ShapeDtypeStruct((total, 8), f32),
        ),
        in_specs=vmem_specs(5),
        out_specs=tuple(vmem_specs(2)),
        scratch_shapes=[pltpu.VMEM((QBLOCK, onehot.shape[1]), f32)],
        compiler_params=pltpu.CompilerParams(vmem_limit_bytes=48 * 2**20),
        cost_estimate=pl.CostEstimate(
            flops=flops, bytes_accessed=8 * total * width, transcendentals=3 * total * total
        ),
        name="attention_forward",
    )(queries, keys, values, table, onehot)


def attention_backward(queries, keys, values, gm, logs, table, onehot):
    total, width = queries.shape
    flops = 10 * total * total * width
    low = jax.ShapeDtypeStruct((total, width), bf16)
    return pl.pallas_call(
        attention_backward_kernel,
        out_shape=(low, low, low, jax.ShapeDtypeStruct((table.shape[0], table.shape[1]), f32)),
        in_specs=vmem_specs(7),
        out_specs=tuple(vmem_specs(4)),
        scratch_shapes=[
            pltpu.VMEM((QBLOCK, onehot.shape[1]), f32),
            pltpu.VMEM((QBLOCK, onehot.shape[1]), f32),
            pltpu.VMEM((8, onehot.shape[1]), f32),
        ],
        compiler_params=pltpu.CompilerParams(vmem_limit_bytes=48 * 2**20),
        cost_estimate=pl.CostEstimate(
            flops=flops, bytes_accessed=14 * total * width, transcendentals=3 * total * total
        ),
        name="attention_backward",
    )(queries, keys, values, gm, logs, table, onehot)


def per_device(
    tokens, gain_attn, pos_table, buckets, w_query, w_key, w_value, w_attn_out, w_router, gain_ffn,
    w_in, w_out, expert_ids, slots, keep, grad_out,
):
    shards = lax.axis_size("shard")
    experts = lax.axis_size("expert")
    me = lax.axis_index("shard")
    block_rows, model_width = tokens.shape[1:]
    total_rows = block_rows * shards
    rows_own = w_query.shape[0]
    local_heads = HEADS // shards
    part_width = local_heads * HEAD_DIM
    expert_count = w_router.shape[1]
    slot_count = expert_count * CAP
    bucket_count = pos_table.shape[0] * shards

    target = jnp.where(keep[0] > 0, expert_ids[0] * CAP + slots[0], -1).astype(jnp.int32)
    small = jnp.concatenate(
        [gain_attn, gain_ffn, pos_table.reshape(-1), w_router.reshape(-1)]
    )
    small_size = small.shape[0]
    small = jnp.pad(small, (0, -small_size % 2048)).reshape(-1, 128)
    small_all = in_order(gather_pairs(small, "shard"), "shard").reshape(shards, -1)
    gain_one = small_all[:, :rows_own].reshape(-1).astype(f32)
    gain_two = small_all[:, rows_own : 2 * rows_own].reshape(-1).astype(f32)
    at = 2 * rows_own
    table_full = small_all[:, at : at + pos_table.size].reshape(bucket_count, HEADS)
    at += pos_table.size
    router_weight = small_all[:, at : at + w_router.size].reshape(model_width, expert_count)

    stacked = jnp.stack([w_query, w_key, w_value], axis=1)
    stacked = stacked.reshape(rows_own, 3, shards, part_width).transpose(2, 0, 1, 3)
    stacked = stacked.reshape(shards, rows_own, 3 * part_width)
    token_blocks = gather_pairs(tokens[0], "shard")
    weight_blocks = [take(stacked, me)]
    for t in range(1, shards):
        weight_blocks.append(swap(take(stacked, partner("shard", t)), "shard", t))
    tokens_all = in_order(token_blocks, "shard").reshape(total_rows, model_width)
    weights = in_order(weight_blocks, "shard").reshape(model_width, 3 * part_width)

    w_attn_out_b, grad_out_b, target_b, _ = lax.optimization_barrier(
        (w_attn_out, grad_out[0], target, weights)
    )
    out_w = gather_pairs(w_attn_out_b, "shard")
    grad_all = in_order(gather_pairs(grad_out_b, "shard"), "shard")
    target_all = in_order(gather_pairs(target_b, "shard"), "shard")

    tokens_all_f = tokens_all.astype(f32)
    normed_all = (tokens_all_f * rms_factor(tokens_all_f) * gain_one).astype(bf16)
    projected = mm(normed_all, weights).astype(bf16)
    queries = projected[:, :part_width]
    keys = projected[:, part_width : 2 * part_width]
    values = projected[:, 2 * part_width :]
    table = lax.dynamic_slice_in_dim(table_full, me * local_heads, local_heads, axis=1)
    table = jnp.pad(table.T, ((0, 8 - local_heads), (0, 0)))
    padded_buckets = jnp.pad(buckets, (0, 2 * total_rows - buckets.shape[0]), constant_values=-1)
    onehot = (padded_buckets[None, :] == jnp.arange(bucket_count)[:, None]).astype(bf16)
    mixed, logs = attention_forward(queries, keys, values, table, onehot)

    mixed_blocks = mixed.reshape(shards, block_rows, part_width)
    mixed_own = [take(mixed_blocks, me)]
    for t in range(1, shards):
        mixed_own.append(swap(take(mixed_blocks, partner("shard", t)), "shard", t))
    tokens_f = tokens[0].astype(f32)
    residual = tokens_f + mm(jnp.concatenate(mixed_own, axis=1), jnp.concatenate(out_w, axis=0))
    normed_two_pre = residual * rms_factor(residual)
    ffn_in = (normed_two_pre * gain_two).astype(bf16)
    router_probs = jax.nn.softmax(mm(ffn_in, router_weight), axis=-1)
    chosen = (expert_ids[0][:, None] == jnp.arange(expert_count)[None, :]).astype(f32)
    gating = jnp.sum(router_probs * chosen, axis=-1, keepdims=True)

    placing = target[None, :] == jnp.arange(slot_count)[:, None]
    placing_low = placing.astype(bf16)
    placing_f = placing.astype(f32)
    grad_y = grad_out[0].astype(f32)
    sent_rows = mm(placing_low, ffn_in).astype(bf16)
    gating_rows = mm_exact(placing_f, gating)
    grad_y_rows = mm(placing_low, grad_out[0])
    sent_grads = (gating_rows * grad_y_rows).astype(bf16)
    sent = jnp.concatenate(
        [
            sent_rows.reshape(expert_count, CAP, model_width),
            sent_grads.reshape(expert_count, CAP, model_width),
        ],
        axis=1,
    )
    sent = jnp.broadcast_to(sent[:, None], (expert_count, shards, 2 * CAP, model_width))
    arrived = lax.all_to_all(
        sent.reshape(expert_count * shards, 2 * CAP, model_width),
        ("expert", "shard"),
        split_axis=0,
        concat_axis=0,
        tiled=True,
    )
    rows_all = arrived[:, :CAP].reshape(-1, model_width)
    grad_rows_all = arrived[:, CAP:].reshape(-1, model_width)
    first_part = w_in[0]
    second_part = w_out[0]
    hidden = mm(rows_all, first_part)
    activation = jax.nn.gelu(hidden).astype(bf16)
    partial_out = mm(activation, second_part).astype(bf16)
    grad_act = mm(grad_rows_all, second_part, NT)
    grad_hidden = gelu_back(hidden, grad_act).astype(bf16)
    grad_partial = mm(grad_hidden, first_part, NT).astype(bf16)
    back = jnp.concatenate(
        [
            partial_out.reshape(-1, CAP, model_width),
            grad_partial.reshape(-1, CAP, model_width),
        ],
        axis=1,
    )
    returned = lax.all_to_all(
        back, ("expert", "shard"), split_axis=0, concat_axis=0, tiled=True
    )
    grad_second = mm(activation, grad_rows_all, TN)
    grad_first = mm(rows_all, grad_hidden, TN)

    kept_all = target_all >= 0
    grad_free = jnp.where(kept_all[..., None], jnp.zeros_like(grad_all), grad_all)
    grad_free = grad_free.reshape(total_rows, model_width)
    mixed_grad_free = mm(grad_free, w_attn_out, NT).astype(bf16)
    placing_all = (
        target_all[:, None, :] == jnp.arange(slot_count)[None, :, None]
    ).astype(bf16)
    mixed_rows = jnp.einsum(
        "bri,bid->brd", placing_all, mixed_blocks, preferred_element_type=f32
    ).astype(bf16)
    residual_rows = mm_exact(placing_f, residual)
    factor_rows = rms_factor(residual_rows)
    normed_rows = residual_rows * factor_rows
    probs_rows = mm_exact(placing_f, router_probs)
    chosen_rows = mm_exact(placing_f, chosen)

    summed = jnp.sum(
        returned.reshape(expert_count, shards, 2 * CAP, model_width).astype(f32), axis=1
    ).astype(bf16)
    out_rows = summed[:, :CAP].reshape(slot_count, model_width)
    grad_back_rows = summed[:, CAP:].reshape(slot_count, model_width).astype(f32)
    output = (residual + gating * mm(placing_low, out_rows, TN)).astype(bf16)
    grad_gate = jnp.sum(grad_y_rows * out_rows.astype(f32), axis=-1, keepdims=True)
    grad_logits = (grad_gate * gating_rows) * (chosen_rows - probs_rows)
    grad_router = mm_exact(sent_rows.astype(f32), grad_logits, TN)
    grad_ffn = grad_back_rows + mm_exact(grad_logits, router_weight.astype(f32), NT)
    grad_gain_two = jnp.sum(grad_ffn * normed_rows, axis=0)
    grad_delta = norm_back(grad_ffn * gain_two, normed_rows, factor_rows)
    att_rows = (grad_y_rows + grad_delta).astype(bf16)
    att_rows_all = in_order(
        [att_rows] + [swap(att_rows, "shard", t) for t in range(1, shards)], "shard"
    )
    mixed_grad_rows = jnp.einsum(
        "brf,cf->brc", att_rows_all, w_attn_out, preferred_element_type=f32
    ).astype(bf16)
    grad_mixed = (
        jnp.einsum("bri,brc->bic", placing_all, mixed_grad_rows, preferred_element_type=f32)
        .astype(bf16)
        .reshape(total_rows, part_width)
        + mixed_grad_free
    )
    grad_out_w = mm(mixed, grad_free, TN) + mm(
        mixed_rows.reshape(-1, part_width), att_rows_all.reshape(-1, model_width), TN
    )

    grad_queries, grad_keys, grad_values, grad_table = attention_backward(
        queries, keys, values, grad_mixed, logs, table, onehot
    )
    grad_projected = jnp.concatenate([grad_queries, grad_keys, grad_values], axis=1)
    grad_weights = mm(normed_all, grad_projected, TN).astype(bf16)

    partial_normed = mm(grad_projected, weights, NT).astype(bf16)
    partial_normed = partial_normed.reshape(shards, block_rows, model_width)
    step = 1
    held = {t: take(partial_normed, partner("shard", t)) for t in range(shards)}
    while len(held) > 1:
        away = [t for t in held if t & step]
        got = swap(jnp.stack([held[t] for t in away]), "shard", step)
        held = {
            t ^ step: (held[t ^ step].astype(f32) + got[i].astype(f32))
            for i, t in enumerate(away)
        }
        if len(held) > 1:
            held = {t: value.astype(bf16) for t, value in held.items()}
        step *= 2
    grad_normed = held[0]
    factor_one = rms_factor(tokens_f)
    grad_residual = grad_y + mm_exact(placing_f, grad_delta, TN)
    grad_tokens = grad_residual + norm_back(grad_normed * gain_one, tokens_f * factor_one, factor_one)

    def total_over_experts(part):
        count, rows, cols = part.shape
        piece = rows // experts
        pieces = part.reshape(count, experts, piece, cols).transpose(1, 0, 2, 3)
        got = lax.all_to_all(
            pieces.reshape(experts, count * piece, cols),
            "expert",
            split_axis=0,
            concat_axis=0,
            tiled=True,
        )
        return jnp.sum(got.astype(f32), axis=0).astype(bf16).reshape(count, piece, cols)

    qkv_sums = total_over_experts(grad_weights.reshape(shards, rows_own, 3 * part_width))
    blocks = [take(qkv_sums, me)]
    for t in range(1, shards):
        blocks.append(swap(take(qkv_sums, partner("shard", t)), "shard", t))
    qkv_mine = in_order(blocks, "shard")
    piece = rows_own // experts
    qkv_mine = (
        qkv_mine.reshape(shards, piece, 3, part_width)
        .transpose(1, 2, 0, 3)
        .reshape(piece, 3 * model_width)
    )
    qkv_total = in_order(gather_pairs(qkv_mine, "expert"), "expert")
    qkv_total = qkv_total.reshape(rows_own, 3, model_width).astype(f32)
    total_query = qkv_total[:, 0]
    total_key = qkv_total[:, 1]
    total_value = qkv_total[:, 2]
    out_sums = total_over_experts(grad_out_w.astype(bf16)[None])
    out_total = in_order(gather_pairs(out_sums[0], "expert"), "expert")
    total_out = out_total.reshape(rows_own, model_width).astype(f32)
    total_one = (
        jnp.sum(
            w_query.astype(f32) * total_query
            + w_key.astype(f32) * total_key
            + w_value.astype(f32) * total_value,
            axis=1,
        )
        / gain_attn.astype(f32)
    )

    router_two = jnp.concatenate([grad_router, grad_gain_two[:, None]], axis=1)
    table_grid = lax.dynamic_update_slice_in_dim(
        jnp.zeros((bucket_count, HEADS), f32),
        grad_table[:local_heads].T,
        me * local_heads,
        axis=1,
    )
    router_two, table_grid = lax.psum((router_two, table_grid), ("expert", "shard"))
    router_two = lax.dynamic_slice_in_dim(router_two, me * rows_own, rows_own, axis=0)
    total_table = lax.dynamic_slice_in_dim(
        table_grid, me * pos_table.shape[0], pos_table.shape[0], axis=0
    )
    return (
        output[None],
        grad_tokens[None],
        total_one,
        total_table,
        total_query,
        total_key,
        total_value,
        total_out,
        router_two[:, :expert_count],
        router_two[:, expert_count],
        grad_first[None],
        grad_second[None],
    )


def solution(mesh):
    in_specs = (
        P("expert", "shard", None),
        P("shard"),
        P("shard", None),
        P(),
        P("shard", None),
        P("shard", None),
        P("shard", None),
        P("shard", None),
        P("shard", None),
        P("shard"),
        P("expert", None, "shard"),
        P("expert", "shard", None),
        P("expert", "shard"),
        P("expert", "shard"),
        P("expert", "shard"),
        P("expert", "shard", None),
    )
    out_specs = (
        P("expert", "shard", None),
        P("expert", "shard", None),
        P("shard"),
        P("shard", None),
        P("shard", None),
        P("shard", None),
        P("shard", None),
        P("shard", None),
        P("shard", None),
        P("shard"),
        P("expert", None, "shard"),
        P("expert", "shard", None),
    )
    return jax.shard_map(
        per_device, mesh=mesh, in_specs=in_specs, out_specs=out_specs, check_vma=False
    )
```

time: 1470 us -> 334 us (0.23)
  local copies, waits for them, and re-layouts: 1030 us -> 62.9 us
  blocking collectives: 141 us -> 40.7 us
  waiting for transfers between devices: 139 us -> 89.5 us
  matrix products: 71.8 us -> 42.3 us
  Pallas kernels: 0 us -> 22.6 us
  starting transfers between devices: 20.9 us -> 41.2 us
  other arithmetic: 42.3 us -> 27.2 us
    gather x2 -> x0, local copies, waits for them, and re-layouts: 942 us -> none  [score_grid(): offset_bias = per_offset[:, offset_index]]
    reduce_scatter x8 -> x0, waiting for transfers between devices: 101 us -> none  [the longest x1 28.3 us: per_device(): lax.psum_scatter(grad_value_w.astype(jnp.bfloat16), 'shard', scatter_dime...]
    ppermute x0 -> x30, waiting for transfers between devices: none -> 77.5 us  [swap(): return lax.ppermute(value, axis, [(i, i ^ bits) for i in range(count)])]
    psum x1, blocking collectives: 101 us -> 40.7 us  [per_device(): lax.psum((router_two, table_grid), ('expert', 'shard'))]
    unnamed x87 -> x104, local copies, waits for them, and re-layouts: 37.6 us -> 3.87 us
    dot_general x33 -> x25, matrix products: 71.8 us -> 42.3 us  [the longest x17 30.6 us: mm(): return lax.dot_general(a, b, dims, preferred_element_type=f32)]
    convert_element_type x3 -> x6, local copies, waits for them, and re-layouts: 33.2 us -> 7.69 us  [the longest x1 2.44 us: per_device(): qkv_total = qkv_total.reshape(rows_own, 3, model_width).astype(f32)]
    all_gather x6 -> x0, waiting for transfers between devices: 23.5 us -> none  [the longest x1 16.3 us: per_device(): lax.all_gather(w_value, 'shard', axis=0, tiled=True)]
  transfers between devices with their start and end apart: 19 -> 34, of which waited for: 11 -> 16; matrix products, arithmetic and copies ran while one was open for 75% -> 23% of each run, Pallas kernels for 0% -> 3%
where the time goes in v1:
time: 334 us; the launch traced here: 328 us
  waiting for transfers between devices  89.5 us (27%)
  local copies, waits for them, and re-layouts  62.9 us (19%)
  matrix products  42.3 us (13%)
  starting transfers between devices  41.2 us (12%)
  blocking collectives  40.7 us (12%)
  other arithmetic  27.2 us (8%)
  Pallas kernels  22.6 us (7%)
    ppermute x30, waiting for transfers between devices, swap(): return lax.ppermute(value, axis, [(i, i ^ bits) for i in range(count)])  77.5 us
    psum x1, blocking collectives, per_device(): lax.psum((router_two, table_grid), ('expert', 'shard'))  40.7 us
    dot_general x17, matrix products, mm(): return lax.dot_general(a, b, dims, preferred_element_type=f32)  30.6 us
    ppermute x30, starting transfers between devices, swap(): return lax.ppermute(value, axis, [(i, i ^ bits) for i in range(count)])  22.2 us
    dynamic_update_slice x42, local copies, waits for them, and re-layouts, in_order(): lax.dynamic_update_slice_in_dim(out, block[None], partner(axis, t), axis=0)  17.4 us
    pallas_call x1, Pallas kernels, attention_backward(): pl.pallas_call(attention_backward_kernel, out_shape=(low, low, low, jax.S...  13.8 us
    all_to_all x2, starting transfers between devices, total_over_experts(): lax.all_to_all(pieces.reshape(experts, count * piece, cols), 'expert', sp...  9.54 us
    dot_general x7, matrix products, mm_exact(): lax.dot_general(a, b, dims, precision=highest, preferred_element_type=f32)  9.15 us
  transfers between devices with their start and end apart: 34, of which 16 were waited for; matrix products, arithmetic and copies ran while one was open for 23% of the time, Pallas kernels for 3%

profile of v1, /device:TPU:0, one launch (start us, length us, event | category | flops | bytes accessed | tf_op | source)
XLA Modules:
  0.0 328.4 jit_solution(3612201773954341169)
XLA Ops:
  5.8 2.5 collective-permute-start.5
  15.5 5.2 %collective-permute-done.2 = bf16[1,16,128]{2,1,0:T(8,128)(2,1)S(1)} collective-permute-done((bf16[1,16,128]{2,1,0:T(8,128)(2,1)S(1)}, bf16[1,16,128]{2,1,0:T(8,128)(2,1)S(1)}, u32[]{:S(2)}, u32[]{:S(2)}) %collective-permute-start.2) | collective-permute-done | bytes 4128 | tf_op jit(solution)/shard_map/ppermute | solution.py:50
  34.6 4.1 %collective-permute-done.12 = s32[1,256]{1,0:T(1,128)S(1)} collective-permute-done((s32[1,256]{1,0:T(1,128)S(1)}, s32[1,256]{1,0:T(1,128)S(1)}, u32[]{:S(2)}, u32[]{:S(2)}) %collective-permute-start.12) | collective-permute-done | bytes 1056 | tf_op jit(solution)/shard_map/ppermute | solution.py:50
  43.3 3.2 collective-permute-done.17
  54.0 2.6 convolution_convert_fusion.1
  56.9 8.8 %attention_forward.1 = (bf16[1024,192]{1,0:T(8,128)(2,1)S(1)}, f32[1024,8]{1,0:T(8,128)S(1)}) custom-call(bf16[1024,192]{1,0:T(8,128)(2,1)S(1)} %get-tuple-element.47.q_ref, bf16[1024,192]{1,0:T(8,128)(2,1)S(1)} %get-tuple-element.46.k_ref, bf16[1024,192]{1,0:T(8,128)(2,1)S(1)} %get-tuple-element.45.v_ref, bf16[8,32]{1,0:T(8,128)(2,1)S(1)} %pad.13.table_ref, ...), custom_call_target="tpu_custom_call" | custom-call | flops 805306368 | bytes 1572864 | tf_op jit(solution)/shard_map/attention_forward/pallas_call | solution.py:175
  71.5 3.0 collective-permute-done.8
  85.7 6.1 %all-to-all-start = ((bf16[32,8,768]{2,1,0:T(8,128)(2,1)}), bf16[32,8,768]{2,1,0:T(8,128)(2,1)}, u32[]{:S(2)}, u32[]{:S(2)}) async-start(bf16[32,8,768]{2,1,0:T(8,128)(2,1)} %bitcast.193), calls=%async_computation | async-start | bytes 786432 | tf_op jit(solution)/shard_map/all_to_all | solution.py:301
  91.8 2.3 multiply_reduce_fusion.5
  97.7 7.3 %all-to-all-done = bf16[32,8,768]{2,1,0:T(8,128)(2,1)} async-done(((bf16[32,8,768]{2,1,0:T(8,128)(2,1)}), bf16[32,8,768]{2,1,0:T(8,128)(2,1)}, u32[]{:S(2)}, u32[]{:S(2)}) %all-to-all-start) | async-done | bytes 393248 | tf_op jit(solution)/shard_map/all_to_all | solution.py:301
  120.9 3.3 %all-to-all-start.1 = ((bf16[32,8,768]{2,1,0:T(8,128)(2,1)}), bf16[32,8,768]{2,1,0:T(8,128)(2,1)}, u32[]{:S(2)}, u32[]{:S(2)}) async-start(bf16[32,8,768]{2,1,0:T(8,128)(2,1)} %pad_maximum_fusion.9), calls=%async_computation.1 | async-start | bytes 786432 | tf_op jit(solution)/shard_map/all_to_all | solution.py:325
  126.0 2.8 broadcast_select_fusion
  132.7 4.7 %all-to-all-done.1 = bf16[32,8,768]{2,1,0:T(8,128)(2,1)} async-done(((bf16[32,8,768]{2,1,0:T(8,128)(2,1)}), bf16[32,8,768]{2,1,0:T(8,128)(2,1)}, u32[]{:S(2)}, u32[]{:S(2)}) %all-to-all-start.1) | async-done | bytes 393248 | tf_op jit(solution)/shard_map/all_to_all | solution.py:325
  155.6 2.5 convolution_convert_fusion.4
  162.2 2.3 fusion.6.gm_ref
  164.5 13.8 %attention_backward.1 = (bf16[1024,192]{1,0:T(8,128)(2,1)S(1)}, bf16[1024,192]{1,0:T(8,128)(2,1)S(1)}, bf16[1024,192]{1,0:T(8,128)(2,1)S(1)}, f32[8,32]{1,0:T(8,128)S(1)}) custom-call(bf16[1024,192]{1,0:T(8,128)(2,1)S(1)} %get-tuple-element.47.q_ref, bf16[1024,192]{1,0:T(8,128)(2,1)S(1)} %get-tuple-element.46.k_ref, ...), custom_call_target="tpu_custom_call" | custom-call | flops 2013265920 | bytes 2752512 | tf_op jit(solution)/shard_map/attention_backward/pallas_call | solution.py:196
  178.3 3.2 convolution_convert_fusion
  184.9 4.1 %all-to-all-start.3 = ((bf16[8,24,768]{2,1,0:T(8,128)(2,1)}), bf16[8,24,768]{2,1,0:T(8,128)(2,1)}, u32[]{:S(2)}, u32[]{:S(2)}) async-start(bf16[8,24,768]{2,1,0:T(8,128)(2,1)} %bitcast.198), calls=%async_computation.3 | async-start | bytes 589824 | tf_op jit(solution)/shard_map/all_to_all | solution.py:405
  189.0 3.7 %convolution_convert_fusion.2 = bf16[768,576]{0,1:T(8,128)(2,1)} fusion(bf16[1024,768]{1,0:T(8,128)(2,1)} %fusion.1, bf16[1024,192]{1,0:T(8,128)(2,1)S(1)} %copy-done.6, bf16[1024,192]{1,0:T(8,128)(2,1)S(1)} %copy-done.4, bf16[1024,192]{1,0:T(8,128)(2,1)S(1)} %copy-done.2), kind=kOutput, calls=%fused_computation.10 | convolution fusion | flops 909950976 | bytes 3637248 | tf_op jit(solution)/shard_map/dot_general | solution.py:27
  195.7 40.7 %all-reduce.3 = (f32[32,12]{1,0:T(8,128)S(1)}, f32[768,9]{0,1:T(8,128)S(1)}) all-reduce(f32[32,12]{1,0:T(8,128)S(1)} %dynamic_update_slice.171, f32[768,9]{0,1:T(8,128)S(1)} %pad_maximum_fusion.14), channel_id=1, replica_groups=mesh['expert'=8,'shard'=4] {'expert','shard'}, use_global_device_ids=true, to_apply=%region_13.14 | all-reduce | flops 7296 | bytes 58368 | tf_op jit(solution)/shard_map/psum | solution.py:450
  236.4 5.5 %all-to-all-start.2 = ((bf16[8,96,576]{2,1,0:T(8,128)(2,1)}), bf16[8,96,576]{2,1,0:T(8,128)(2,1)S(1)}, u32[]{:S(2)}, u32[]{:S(2)}) async-start(bf16[8,96,576]{2,1,0:T(8,128)(2,1)} %bitcast.53), calls=%async_computation.2 | async-start | bytes 1966080 | tf_op jit(solution)/shard_map/all_to_all | solution.py:405
  242.9 3.0 collective-permute-start.27
  247.2 19.6 %collective-permute-done.27 = bf16[1,24,768]{2,1,0:T(8,128)(2,1)S(1)} collective-permute-done((bf16[1,24,768]{2,1,0:T(8,128)(2,1)S(1)}, bf16[1,24,768]{2,1,0:T(8,128)(2,1)S(1)}, u32[]{:S(2)}, u32[]{:S(2)}) %collective-permute-start.27) | collective-permute-done | bytes 36896 | tf_op jit(solution)/shard_map/ppermute | solution.py:50
  267.5 3.7 %collective-permute-done.28 = bf16[2,24,768]{2,1,0:T(8,128)(2,1)S(1)} collective-permute-done((bf16[2,24,768]{2,1,0:T(8,128)(2,1)S(1)}, bf16[2,24,768]{2,1,0:T(8,128)(2,1)S(1)}, u32[]{:S(2)}, u32[]{:S(2)}) %collective-permute-start.28) | collective-permute-done | bytes 73760 | tf_op jit(solution)/shard_map/ppermute | solution.py:50
  272.6 3.9 %collective-permute-done.29 = bf16[4,24,768]{2,1,0:T(8,128)(2,1)S(1)} collective-permute-done((bf16[4,24,768]{2,1,0:T(8,128)(2,1)S(1)}, bf16[4,24,768]{2,1,0:T(8,128)(2,1)S(1)}, u32[]{:S(2)}, u32[]{:S(2)}) %collective-permute-start.29) | collective-permute-done | bytes 147488 | tf_op jit(solution)/shard_map/ppermute | solution.py:50
  281.5 10.0 %collective-permute-done.22 = bf16[24,576]{1,0:T(8,128)(2,1)S(1)} collective-permute-done((bf16[24,576]{1,0:T(8,128)(2,1)S(1)}, bf16[24,576]{1,0:T(8,128)(2,1)S(1)}, u32[]{:S(2)}, u32[]{:S(2)}) %collective-permute-start.22) | collective-permute-done | bytes 27680 | tf_op jit(solution)/shard_map/ppermute | solution.py:50
  293.6 6.3 %collective-permute-done.24 = bf16[1,24,2304]{2,1,0:T(8,128)(2,1)S(1)} collective-permute-done((bf16[1,24,2304]{2,1,0:T(8,128)(2,1)S(1)}, bf16[1,24,2304]{2,1,0:T(8,128)(2,1)S(1)}, u32[]{:S(2)}, u32[]{:S(2)}) %collective-permute-start.24) | collective-permute-done | bytes 110624 | tf_op jit(solution)/shard_map/ppermute | solution.py:50
  300.0 7.3 %collective-permute-done.25 = bf16[2,24,2304]{2,1,0:T(8,128)(2,1)S(1)} collective-permute-done((bf16[2,24,2304]{2,1,0:T(8,128)(2,1)S(1)}, bf16[2,24,2304]{2,1,0:T(8,128)(2,1)S(1)}, u32[]{:S(2)}, u32[]{:S(2)}) %collective-permute-start.25) | collective-permute-done | bytes 221216 | tf_op jit(solution)/shard_map/ppermute | solution.py:50
  308.7 2.8 fusion.4
  311.6 7.2 %collective-permute-done.26 = bf16[4,24,2304]{2,1,0:T(8,128)(2,1)S(1)} collective-permute-done((bf16[4,24,2304]{2,1,0:T(8,128)(2,1)S(1)}, bf16[4,24,2304]{2,1,0:T(8,128)(2,1)S(1)}, u32[]{:S(2)}, u32[]{:S(2)}) %collective-permute-start.26) | collective-permute-done | bytes 442400 | tf_op jit(solution)/shard_map/ppermute | solution.py:50
  318.9 2.4 reshape.246
  321.3 4.9 %fusion.80 = (f32[192,1,768]{2,1,0:T(1,128)S(1)}, f32[192,1,768]{2,1,0:T(1,128)S(1)}, f32[192,1,768]{2,1,0:T(1,128)S(1)}) fusion(f32[192,3,768]{2,1,0:T(4,128)} %reshape.246), kind=kLoop, calls=%fused_computation.212 | loop fusion | bytes 3538944 | tf_op jit(solution)/shard_map/slice | solution.py:429
  (317 shorter events, 123.6 us)
Async XLA Ops:
  4.5 18.9 %collective-permute-start.4 = (bf16[192,576]{1,0:T(8,128)(2,1)}, bf16[192,576]{1,0:T(8,128)(2,1)}, u32[]{:S(2)}, u32[]{:S(2)}) collective-permute-start(bf16[192,576]{1,0:T(8,128)(2,1)} %bitcast.9), channel_id=1, source_target_pairs={{0,1},{1,0},{2,3},{3,2},{4,5},{5,4},{6,7},{7,6},{8,9},{9,8},{10,11... | collective-permute-start | bytes 663560 | tf_op jit(solution)/shard_map/ppermute | solution.py:50
  5.8 19.3 %collective-permute-start.5 = (bf16[192,576]{1,0:T(8,128)(2,1)}, bf16[192,576]{1,0:T(8,128)(2,1)}, u32[]{:S(2)}, u32[]{:S(2)}) collective-permute-start(bf16[192,576]{1,0:T(8,128)(2,1)} %bitcast.11), channel_id=1, source_target_pairs={{0,2},{1,3},{2,0},{3,1},{4,6},{5,7},{6,4},{7,5},{8,10},{9,11},{10,... | collective-permute-start | bytes 663560 | tf_op jit(solution)/shard_map/ppermute | solution.py:50
  9.2 17.7 %collective-permute-start.6 = (bf16[192,576]{1,0:T(8,128)(2,1)}, bf16[192,576]{1,0:T(8,128)(2,1)}, u32[]{:S(2)}, u32[]{:S(2)}) collective-permute-start(bf16[192,576]{1,0:T(8,128)(2,1)} %bitcast.13), channel_id=1, source_target_pairs={{0,3},{1,2},{2,1},{3,0},{4,7},{5,6},{6,5},{7,4},{8,11},{9,10},{10,... | collective-permute-start | bytes 663560 | tf_op jit(solution)/shard_map/ppermute | solution.py:50
  9.8 10.9 %collective-permute-start.2 = (bf16[1,16,128]{2,1,0:T(8,128)(2,1)S(1)}, bf16[1,16,128]{2,1,0:T(8,128)(2,1)S(1)}, u32[]{:S(2)}, u32[]{:S(2)}) collective-permute-start(bf16[1,16,128]{2,1,0:T(8,128)(2,1)S(1)} %pad_bitcast_fusion), channel_id=1, source_target_pairs={{0,2},{1,3},{2,0},{3,1},{4,6},{5,7},{6,4},{7,5},{8,10},{9,11},{10,... | collective-permute-start | bytes 12296 | tf_op jit(solution)/shard_map/ppermute | solution.py:50
  11.6 29.5 %collective-permute-start = (bf16[1,256,768]{2,1,0:T(8,128)(2,1)S(1)}, bf16[1,256,768]{2,1,0:T(8,128)(2,1)}, u32[]{:S(2)}, u32[]{:S(2)}) collective-permute-start(bf16[1,256,768]{2,1,0:T(8,128)(2,1)S(1)} %copy-done.13), channel_id=1, source_target_pairs={{0,2},{1,3},{2,0},{3,1},{4,6},{5,7},{6,4},{7,5},{8,10},{9,11},{10,... | collective-permute-start | bytes 1179656 | tf_op jit(solution)/shard_map/ppermute | solution.py:50
  28.5 10.2 %collective-permute-start.10 = (bf16[1,192,768]{2,1,0:T(8,128)(2,1)}, bf16[1,192,768]{2,1,0:T(8,128)(2,1)}, u32[]{:S(2)}, u32[]{:S(2)}) collective-permute-start(bf16[1,192,768]{2,1,0:T(8,128)(2,1)} %bitcast.199), channel_id=1, source_target_pairs={{0,2},{1,3},{2,0},{3,1},{4,6},{5,7},{6,4},{7,5},{8,10},{9,11},{10,... | collective-permute-start | bytes 884744 | tf_op jit(solution)/shard_map/ppermute | solution.py:50
  30.4 8.2 %collective-permute-start.12 = (s32[1,256]{1,0:T(1,128)S(1)}, s32[1,256]{1,0:T(1,128)S(1)}, u32[]{:S(2)}, u32[]{:S(2)}) collective-permute-start(s32[1,256]{1,0:T(1,128)S(1)} %bitcast.223), channel_id=1, source_target_pairs={{0,2},{1,3},{2,0},{3,1},{4,6},{5,7},{6,4},{7,5},{8,10},{9,11},{10,... | collective-permute-start | bytes 3080 | tf_op jit(solution)/shard_map/ppermute | solution.py:50
  32.6 14.0 %collective-permute-start.17 = (bf16[1,256,768]{2,1,0:T(8,128)(2,1)}, bf16[1,256,768]{2,1,0:T(8,128)(2,1)}, u32[]{:S(2)}, u32[]{:S(2)}) collective-permute-start(bf16[1,256,768]{2,1,0:T(8,128)(2,1)} %param.31), channel_id=1, source_target_pairs={{0,2},{1,3},{2,0},{3,1},{4,6},{5,7},{6,4},{7,5},{8,10},{9,11},{10,... | collective-permute-start | bytes 1179656 | tf_op jit(solution)/shard_map/ppermute | solution.py:50
  38.6 4.4 %collective-permute-start.13 = (s32[2,256]{1,0:T(2,128)S(1)}, s32[2,256]{1,0:T(2,128)S(1)}, u32[]{:S(2)}, u32[]{:S(2)}) collective-permute-start(s32[2,256]{1,0:T(2,128)S(1)} %pad_add_fusion), channel_id=1, source_target_pairs={{0,1},{1,0},{2,3},{3,2},{4,5},{5,4},{6,7},{7,6},{8,9},{9,8},{10,11... | collective-permute-start | bytes 6152 | tf_op jit(solution)/shard_map/ppermute | solution.py:50
  40.6 8.0 %collective-permute-start.11 = (bf16[2,192,768]{2,1,0:T(8,128)(2,1)}, bf16[2,192,768]{2,1,0:T(8,128)(2,1)}, u32[]{:S(2)}, u32[]{:S(2)}) collective-permute-start(bf16[2,192,768]{2,1,0:T(8,128)(2,1)} %pad_maximum_fusion.5), channel_id=1, source_target_pairs={{0,1},{1,0},{2,3},{3,2},{4,5},{5,4},{6,7},{7,6},{8,9},{9,8},{10,11... | collective-permute-start | bytes 1769480 | tf_op jit(solution)/shard_map/ppermute | solution.py:50
  43.0 6.7 %collective-permute-start.1 = (bf16[2,256,768]{2,1,0:T(8,128)(2,1)}, bf16[2,256,768]{2,1,0:T(8,128)(2,1)}, u32[]{:S(2)}, u32[]{:S(2)}) collective-permute-start(bf16[2,256,768]{2,1,0:T(8,128)(2,1)} %pad_maximum_fusion.2), channel_id=1, source_target_pairs={{0,1},{1,0},{2,3},{3,2},{4,5},{5,4},{6,7},{7,6},{8,9},{9,8},{10,11... | collective-permute-start | bytes 2359304 | tf_op jit(solution)/shard_map/ppermute | solution.py:50
  48.6 45.5 %collective-permute-start.18 = (bf16[2,256,768]{2,1,0:T(8,128)(2,1)}, bf16[2,256,768]{2,1,0:T(8,128)(2,1)}, u32[]{:S(2)}, u32[]{:S(2)}) collective-permute-start(bf16[2,256,768]{2,1,0:T(8,128)(2,1)} %pad_maximum_fusion.3), channel_id=1, source_target_pairs={{0,1},{1,0},{2,3},{3,2},{4,5},{5,4},{6,7},{7,6},{8,9},{9,8},{10,11... | collective-permute-start | bytes 2359304 | tf_op jit(solution)/shard_map/ppermute | solution.py:50
  65.7 5.8 %collective-permute-start.9 = (bf16[256,192]{1,0:T(8,128)(2,1)S(1)}, bf16[256,192]{1,0:T(8,128)(2,1)S(1)}, u32[]{:S(2)}, u32[]{:S(2)}) collective-permute-start(bf16[256,192]{1,0:T(8,128)(2,1)S(1)} %get-tuple-element.55), channel_id=1, source_target_pairs={{0,3},{1,2},{2,1},{3,0},{4,7},{5,6},{6,5},{7,4},{8,11},{9,10},{10,... | collective-permute-start | bytes 294920 | tf_op jit(solution)/shard_map/ppermute | solution.py:50
  67.7 6.9 %collective-permute-start.8 = (bf16[256,192]{1,0:T(8,128)(2,1)S(1)}, bf16[256,192]{1,0:T(8,128)(2,1)S(1)}, u32[]{:S(2)}, u32[]{:S(2)}) collective-permute-start(bf16[256,192]{1,0:T(8,128)(2,1)S(1)} %get-tuple-element.56), channel_id=1, source_target_pairs={{0,2},{1,3},{2,0},{3,1},{4,6},{5,7},{6,4},{7,5},{8,10},{9,11},{10,... | collective-permute-start | bytes 294920 | tf_op jit(solution)/shard_map/ppermute | solution.py:50
  68.0 6.6 %collective-permute-start.7 = (bf16[256,192]{1,0:T(8,128)(2,1)S(1)}, bf16[256,192]{1,0:T(8,128)(2,1)S(1)}, u32[]{:S(2)}, u32[]{:S(2)}) collective-permute-start(bf16[256,192]{1,0:T(8,128)(2,1)S(1)} %get-tuple-element.57), channel_id=1, source_target_pairs={{0,1},{1,0},{2,3},{3,2},{4,5},{5,4},{6,7},{7,6},{8,9},{9,8},{10,11... | collective-permute-start | bytes 294920 | tf_op jit(solution)/shard_map/ppermute | solution.py:50
  85.7 19.3 %all-to-all-start = ((bf16[32,8,768]{2,1,0:T(8,128)(2,1)}), bf16[32,8,768]{2,1,0:T(8,128)(2,1)}, u32[]{:S(2)}, u32[]{:S(2)}) async-start(bf16[32,8,768]{2,1,0:T(8,128)(2,1)} %bitcast.193), calls=%async_computation | async-start | bytes 786432 | tf_op jit(solution)/shard_map/all_to_all | solution.py:301
  120.9 16.5 %all-to-all-start.1 = ((bf16[32,8,768]{2,1,0:T(8,128)(2,1)}), bf16[32,8,768]{2,1,0:T(8,128)(2,1)}, u32[]{:S(2)}, u32[]{:S(2)}) async-start(bf16[32,8,768]{2,1,0:T(8,128)(2,1)} %pad_maximum_fusion.9), calls=%async_computation.1 | async-start | bytes 786432 | tf_op jit(solution)/shard_map/all_to_all | solution.py:325
  149.9 4.4 %collective-permute-start.15 = (bf16[32,768]{1,0:T(8,128)(2,1)S(1)}, bf16[32,768]{1,0:T(8,128)(2,1)S(1)}, u32[]{:S(2)}, u32[]{:S(2)}) collective-permute-start(bf16[32,768]{1,0:T(8,128)(2,1)S(1)} %get-tuple-element.39), channel_id=1, source_target_pairs={{0,2},{1,3},{2,0},{3,1},{4,6},{5,7},{6,4},{7,5},{8,10},{9,11},{10,... | collective-permute-start | bytes 147464 | tf_op jit(solution)/shard_map/ppermute | solution.py:50
  150.9 4.0 %collective-permute-start.16 = (bf16[32,768]{1,0:T(8,128)(2,1)S(1)}, bf16[32,768]{1,0:T(8,128)(2,1)S(1)}, u32[]{:S(2)}, u32[]{:S(2)}) collective-permute-start(bf16[32,768]{1,0:T(8,128)(2,1)S(1)} %get-tuple-element.39), channel_id=1, source_target_pairs={{0,3},{1,2},{2,1},{3,0},{4,7},{5,6},{6,5},{7,4},{8,11},{9,10},{10,... | collective-permute-start | bytes 147464 | tf_op jit(solution)/shard_map/ppermute | solution.py:50
  183.6 94.2 %collective-permute-start.19 = (bf16[2,256,768]{2,1,0:T(8,128)(2,1)}, bf16[2,256,768]{2,1,0:T(8,128)(2,1)}, u32[]{:S(2)}, u32[]{:S(2)}) collective-permute-start(bf16[2,256,768]{2,1,0:T(8,128)(2,1)} %pad_maximum_fusion.4), channel_id=1, source_target_pairs={{0,1},{1,0},{2,3},{3,2},{4,5},{5,4},{6,7},{7,6},{8,9},{9,8},{10,11... | collective-permute-start | bytes 2359304 | tf_op jit(solution)/shard_map/ppermute | solution.py:50
  184.9 51.4 %all-to-all-start.3 = ((bf16[8,24,768]{2,1,0:T(8,128)(2,1)}), bf16[8,24,768]{2,1,0:T(8,128)(2,1)}, u32[]{:S(2)}, u32[]{:S(2)}) async-start(bf16[8,24,768]{2,1,0:T(8,128)(2,1)} %bitcast.198), calls=%async_computation.3 | async-start | bytes 589824 | tf_op jit(solution)/shard_map/all_to_all | solution.py:405
  236.4 41.1 %all-to-all-start.2 = ((bf16[8,96,576]{2,1,0:T(8,128)(2,1)}), bf16[8,96,576]{2,1,0:T(8,128)(2,1)S(1)}, u32[]{:S(2)}, u32[]{:S(2)}) async-start(bf16[8,96,576]{2,1,0:T(8,128)(2,1)} %bitcast.53), calls=%async_computation.2 | async-start | bytes 1966080 | tf_op jit(solution)/shard_map/all_to_all | solution.py:405
  242.9 23.9 %collective-permute-start.27 = (bf16[1,24,768]{2,1,0:T(8,128)(2,1)S(1)}, bf16[1,24,768]{2,1,0:T(8,128)(2,1)S(1)}, u32[]{:S(2)}, u32[]{:S(2)}) collective-permute-start(bf16[1,24,768]{2,1,0:T(8,128)(2,1)S(1)} %bitcast.202), channel_id=1, source_target_pairs={{0,16},{4,20},{8,24},{12,28},{16,0},{20,4},{24,8},{28,12},{1,17},{... | collective-permute-start | bytes 110600 | tf_op jit(solution)/shard_map/ppermute | solution.py:50
  266.8 4.4 %collective-permute-start.28 = (bf16[2,24,768]{2,1,0:T(8,128)(2,1)S(1)}, bf16[2,24,768]{2,1,0:T(8,128)(2,1)S(1)}, u32[]{:S(2)}, u32[]{:S(2)}) collective-permute-start(bf16[2,24,768]{2,1,0:T(8,128)(2,1)S(1)} %pad_maximum_fusion.13), channel_id=1, source_target_pairs={{0,8},{4,12},{8,0},{12,4},{16,24},{20,28},{24,16},{28,20},{1,9},{5... | collective-permute-start | bytes 221192 | tf_op jit(solution)/shard_map/ppermute | solution.py:50
  271.2 5.2 %collective-permute-start.29 = (bf16[4,24,768]{2,1,0:T(8,128)(2,1)S(1)}, bf16[4,24,768]{2,1,0:T(8,128)(2,1)S(1)}, u32[]{:S(2)}, u32[]{:S(2)}) collective-permute-start(bf16[4,24,768]{2,1,0:T(8,128)(2,1)S(1)} %pad_maximum_fusion.11), channel_id=1, source_target_pairs={{0,4},{4,0},{8,12},{12,8},{16,20},{20,16},{24,28},{28,24},{1,5},{5... | collective-permute-start | bytes 442376 | tf_op jit(solution)/shard_map/ppermute | solution.py:50
  277.7 3.8 %collective-permute-start.21 = (bf16[24,576]{1,0:T(8,128)(2,1)S(1)}, bf16[24,576]{1,0:T(8,128)(2,1)S(1)}, u32[]{:S(2)}, u32[]{:S(2)}) collective-permute-start(bf16[24,576]{1,0:T(8,128)(2,1)S(1)} %get-tuple-element.62), channel_id=1, source_target_pairs={{0,1},{1,0},{2,3},{3,2},{4,5},{5,4},{6,7},{7,6},{8,9},{9,8},{10,11... | collective-permute-start | bytes 82952 | tf_op jit(solution)/shard_map/ppermute | solution.py:50
  279.0 13.1 %collective-permute-start.20 = (bf16[1,256,768]{2,1,0:T(8,128)(2,1)S(1)}, bf16[1,256,768]{2,1,0:T(8,128)(2,1)S(1)}, u32[]{:S(2)}, u32[]{:S(2)}) collective-permute-start(bf16[1,256,768]{2,1,0:T(8,128)(2,1)S(1)} %add_convert_fusion), channel_id=1, source_target_pairs={{0,2},{1,3},{2,0},{3,1},{4,6},{5,7},{6,4},{7,5},{8,10},{9,11},{10,... | collective-permute-start | bytes 1179656 | tf_op jit(solution)/shard_map/ppermute | solution.py:50
  280.0 11.6 %collective-permute-start.22 = (bf16[24,576]{1,0:T(8,128)(2,1)S(1)}, bf16[24,576]{1,0:T(8,128)(2,1)S(1)}, u32[]{:S(2)}, u32[]{:S(2)}) collective-permute-start(bf16[24,576]{1,0:T(8,128)(2,1)S(1)} %get-tuple-element.61), channel_id=1, source_target_pairs={{0,2},{1,3},{2,0},{3,1},{4,6},{5,7},{6,4},{7,5},{8,10},{9,11},{10,... | collective-permute-start | bytes 82952 | tf_op jit(solution)/shard_map/ppermute | solution.py:50
  281.1 10.5 %collective-permute-start.23 = (bf16[24,576]{1,0:T(8,128)(2,1)S(1)}, bf16[24,576]{1,0:T(8,128)(2,1)S(1)}, u32[]{:S(2)}, u32[]{:S(2)}) collective-permute-start(bf16[24,576]{1,0:T(8,128)(2,1)S(1)} %get-tuple-element.60), channel_id=1, source_target_pairs={{0,3},{1,2},{2,1},{3,0},{4,7},{5,6},{6,5},{7,4},{8,11},{9,10},{10,... | collective-permute-start | bytes 82952 | tf_op jit(solution)/shard_map/ppermute | solution.py:50
  292.0 7.9 %collective-permute-start.24 = (bf16[1,24,2304]{2,1,0:T(8,128)(2,1)S(1)}, bf16[1,24,2304]{2,1,0:T(8,128)(2,1)S(1)}, u32[]{:S(2)}, u32[]{:S(2)}) collective-permute-start(bf16[1,24,2304]{2,1,0:T(8,128)(2,1)S(1)} %broadcast_in_dim_reshape.7), channel_id=1, source_target_pairs={{0,16},{4,20},{8,24},{12,28},{16,0},{20,4},{24,8},{28,12},{1,17},{... | collective-permute-start | bytes 331784 | tf_op jit(solution)/shard_map/ppermute | solution.py:50
  299.9 7.4 %collective-permute-start.25 = (bf16[2,24,2304]{2,1,0:T(8,128)(2,1)S(1)}, bf16[2,24,2304]{2,1,0:T(8,128)(2,1)S(1)}, u32[]{:S(2)}, u32[]{:S(2)}) collective-permute-start(bf16[2,24,2304]{2,1,0:T(8,128)(2,1)S(1)} %pad_maximum_fusion.10), channel_id=1, source_target_pairs={{0,8},{4,12},{8,0},{12,4},{16,24},{20,28},{24,16},{28,20},{1,9},{5... | collective-permute-start | bytes 663560 | tf_op jit(solution)/shard_map/ppermute | solution.py:50
  307.4 11.3 %collective-permute-start.26 = (bf16[4,24,2304]{2,1,0:T(8,128)(2,1)S(1)}, bf16[4,24,2304]{2,1,0:T(8,128)(2,1)S(1)}, u32[]{:S(2)}, u32[]{:S(2)}) collective-permute-start(bf16[4,24,2304]{2,1,0:T(8,128)(2,1)S(1)} %pad_maximum_fusion.6), channel_id=1, source_target_pairs={{0,4},{4,0},{8,12},{12,8},{16,20},{20,16},{24,28},{28,24},{1,5},{5... | collective-permute-start | bytes 1327112 | tf_op jit(solution)/shard_map/ppermute | solution.py:50
  (52 other events, 368.2 us)
